TPU v7x, 32 devices: a whole 2x2x4 slice. The times are simulated.
32 devices in a mesh: req: 2 (over x), blk: 16 (over z, y, core).
Axes of the slice: x: 2, y: 2, z: 4, core: 2. Of those that a mesh axis runs over, the one named last changes fastest.
Arguments:
- tokens: bfloat16 [32, 128, 1536], P(('req', 'blk')), may hold values from -6 to 6
- cache_kv: bfloat16 [32, 2, 256, 384], P(('req', 'blk')), may hold values from -200 to 200
- cache_len: int32 [32], P(('req', 'blk')), may hold values from 2 to 256, as said below
- holder: int32 [32], P(('req', 'blk')), may hold values from 0 to 1, as said below
- accept: int32 [32, 128], P(('req', 'blk')), may hold values from 0 to 1, as said below
- attn_gain: float32 [1536], replicated, may hold values from 0.1 to 1.9
- q_weight: bfloat16 [1536, 768], replicated, may hold values from -0.15625 to 0.15625
- k_weight: bfloat16 [1536, 384], replicated, may hold values from -0.15625 to 0.15625
- v_weight: bfloat16 [1536, 384], replicated, may hold values from -0.15625 to 0.15625
- o_weight: bfloat16 [768, 1536], replicated, may hold values from -0.21875 to 0.21875
- ffn_gain: float32 [1536], replicated, may hold values from 0.4 to 2.5
- w_gate: bfloat16 [1536, 4096], P(None, 'blk'), may hold values from -0.15625 to 0.15625
- w_up: bfloat16 [1536, 4096], P(None, 'blk'), may hold values from -0.15625 to 0.15625
- w_down: bfloat16 [4096, 1536], P('blk'), may hold values from -0.09375 to 0.09375
Outputs:
- refined: float32 [32, 128, 1536], P(('req', 'blk'))
Inputs may be any that keep to these rules, and one draw needn't show every extreme that they name: `holder`: requests whose numbers agree modulo 16 have distinct holders. `cache_len`: some request has exactly 256 cached positions. `accept`: each request accepts exactly 64 positions.
All inputs are finite; a program needn't handle non-finite values.
Results may differ from a plain program's by a relative error of at most 0.04.
Values may be sent and summed in bfloat16 or wider, within the bound.
A program may use at most 128 MiB of HBM per device.

v0:
```python
import jax
import jax.numpy as jnp
from jax import lax
from jax.sharding import PartitionSpec as P

HEAD = 96


norm_eps = 1e-05
rope_base = 100000.0


def rms_scale(values, gain_row):
    return (
        values * lax.rsqrt(jnp.mean(values * values, axis=-1, keepdims=True) + norm_eps) * gain_row
    )


def rotate_heads(flat, positions, head_count):
    half_dim = HEAD // 2
    shaped = flat.reshape(flat.shape[0], head_count, HEAD)
    freqs = jnp.exp(-jnp.log(rope_base) * 2.0 * jnp.arange(half_dim, dtype=jnp.float32) / HEAD)
    angles = positions[:, None] * freqs[None, :]
    cosine = jnp.cos(angles)[:, None, :]
    sine = jnp.sin(angles)[:, None, :]
    first_half = shaped[..., :half_dim]
    second_half = shaped[..., half_dim:]
    turned = jnp.concatenate(
        [first_half * cosine - second_half * sine, second_half * cosine + first_half * sine],
        axis=-1,
    )
    return turned.reshape(flat.shape[0], head_count * HEAD)


def attend_block(
    tok_rows,
    cache_keys,
    cache_vals,
    cache_length,
    attn_gain,
    q_weight,
    k_weight,
    v_weight,
    o_weight,
):
    block_len = tok_rows.shape[0]
    slot_len = cache_keys.shape[0]
    kv_count = k_weight.shape[1] // HEAD
    q_count = q_weight.shape[1] // HEAD
    widened = tok_rows.astype(jnp.float32)
    normed = rms_scale(widened, attn_gain).astype(jnp.bfloat16)
    positions = (cache_length + jnp.arange(block_len, dtype=jnp.int32)).astype(jnp.float32)
    queries = rotate_heads(
        jnp.dot(normed, q_weight, preferred_element_type=jnp.float32), positions, q_count
    ).astype(jnp.bfloat16)
    new_keys = rotate_heads(
        jnp.dot(normed, k_weight, preferred_element_type=jnp.float32), positions, kv_count
    ).astype(jnp.bfloat16)
    new_vals = jnp.dot(normed, v_weight, preferred_element_type=jnp.float32).astype(jnp.bfloat16)
    all_keys = jnp.concatenate([cache_keys, new_keys], axis=0).reshape(
        slot_len + block_len, kv_count, HEAD
    )
    all_vals = jnp.concatenate([cache_vals, new_vals], axis=0).reshape(
        slot_len + block_len, kv_count, HEAD
    )
    grouped = queries.reshape(block_len, kv_count, q_count // kv_count, HEAD)
    scores = jnp.einsum(
        "bgid,kgd->gibk", grouped, all_keys, preferred_element_type=jnp.float32
    ) * HEAD ** (-0.5)
    valid = jnp.concatenate(
        [
            jnp.arange(slot_len, dtype=jnp.int32) < cache_length,
            jnp.ones((block_len,), dtype=jnp.bool_),
        ]
    )
    scores = jnp.where(valid, scores, -jnp.inf)
    peaks = jnp.max(scores, axis=-1, keepdims=True)
    expd = jnp.exp(scores - peaks)
    probs = (expd / jnp.sum(expd, axis=-1, keepdims=True)).astype(jnp.bfloat16)
    context = jnp.einsum("gibk,kgd->bgid", probs, all_vals, preferred_element_type=jnp.float32)
    context = context.astype(jnp.bfloat16).reshape(block_len, q_count * HEAD)
    return widened + jnp.dot(context, o_weight, preferred_element_type=jnp.float32)


def run_ffn(normed_rows, w_gate, w_up, w_down):
    part_rows = lax.all_gather(normed_rows, "blk", axis=0, tiled=True)
    gate_vals = jnp.dot(part_rows, w_gate, preferred_element_type=jnp.float32)
    up_vals = jnp.dot(part_rows, w_up, preferred_element_type=jnp.float32)
    hidden_all = (jax.nn.silu(gate_vals) * up_vals).astype(jnp.bfloat16)
    return lax.psum_scatter(
        jnp.dot(hidden_all, w_down, preferred_element_type=jnp.float32).astype(jnp.bfloat16),
        "blk",
        scatter_dimension=0,
        tiled=True,
    ).astype(jnp.float32)


def local(
    tokens,
    cache_kv,
    cache_len,
    holder,
    accept,
    attn_gain,
    q_weight,
    k_weight,
    v_weight,
    o_weight,
    ffn_gain,
    w_gate,
    w_up,
    w_down,
):
    own_holder = holder[0]
    part_rows = lax.all_gather(cache_kv, "req", axis=0, tiled=True)
    matches = jnp.arange(part_rows.shape[0], dtype=jnp.int32) == own_holder
    fetched = jnp.sum(
        jnp.where(matches[:, None, None, None], part_rows, jnp.zeros_like(part_rows)), axis=0
    )
    cache_keys = fetched[0]
    cache_vals = fetched[1]
    cache_length = cache_len[0]
    block_rows = tokens[0]
    first_pass = attend_block(
        block_rows,
        cache_keys,
        cache_vals,
        cache_length,
        attn_gain,
        q_weight,
        k_weight,
        v_weight,
        o_weight,
    )
    chosen_mask = accept[0] == 1
    ffn_sum = run_ffn(rms_scale(first_pass, ffn_gain).astype(jnp.bfloat16), w_gate, w_up, w_down)
    placed = first_pass + ffn_sum
    second_in = jnp.where(chosen_mask[:, None], placed, block_rows.astype(jnp.float32))
    refined = attend_block(
        second_in,
        cache_keys,
        cache_vals,
        cache_length,
        attn_gain,
        q_weight,
        k_weight,
        v_weight,
        o_weight,
    )
    return refined[None]


def solution(mesh):
    return jax.shard_map(
        local,
        mesh=mesh,
        in_specs=(
            P(("req", "blk"), None, None),
            P(("req", "blk"), None, None, None),
            P(("req", "blk")),
            P(("req", "blk")),
            P(("req", "blk"), None),
            P(),
            P(),
            P(),
            P(),
            P(),
            P(),
            P(None, "blk"),
            P(None, "blk"),
            P("blk", None),
        ),
        out_specs=P(("req", "blk"), None, None),
        check_vma=False,
    )
```

profile of v0, /device:TPU:0, one launch (start us, length us, event | category | flops | bytes accessed | tf_op | source)
XLA Modules:
  0.0 231.8 jit_solution(12172445451921997107)
XLA Ops:
  6.5 0.0 copy-start
  6.5 0.0 all-gather.2.cloned.1.call-start
  7.4 1.2 fusion.18
  8.5 4.3 %copy.35 = bf16[1536,768]{0,1:T(8,128)(2,1)} copy(bf16[1536,768]{1,0:T(8,128)(2,1)} %param.20) | data formatting | bytes 4718592 | tf_op args[6]
  12.8 2.5 %copy.34 = bf16[1536,384]{0,1:T(8,128)(2,1)} copy(bf16[1536,384]{1,0:T(8,128)(2,1)} %param.21) | data formatting | bytes 2359296 | tf_op args[7]
  15.3 0.0 copy-done.1
  15.3 0.0 copy-done.16
  15.3 2.6 %fusion.51 = f32[128,8,96]{0,2,1:T(8,128)S(1)} fusion(bf16[8,96,1536]{2,1,0:T(8,128)(2,1)} %bitcast.124, bf16[1,128,1536]{2,1,0:T(8,128)(2,1)S(1)} %copy-done.1, f32[1536]{0:T(1024)S(1)} %copy-done.16, f32[128]{0:T(128)S(1)} %add_rsqrt_fusion.2), kind=kOutput, calls=%fused_computation.65 | convolution fusion | flops 302776320 | bytes 3152384 | tf_op jit(solution)/shard_map/dot_general | solution.py:54
  17.9 0.0 copy-start.11
  17.9 0.0 copy-done.5
  17.9 0.5 fusion.53
  18.4 0.2 multiply_cosine_fusion
  18.6 0.0 copy-start.7
  18.6 0.0 copy-start.9
  18.6 0.1 subtract_convert_fusion.1
  18.7 0.7 subtract_convert_fusion.3
  19.4 0.0 copy-done.11
  19.4 12.7 %all_gather.6 = bf16[2,2,256,384]{3,2,1,0:T(8,128)(2,1)S(1)} all-gather(bf16[1,2,256,384]{3,2,1,0:T(8,128)(2,1)S(1)} %copy-done.11), channel_id=1, replica_groups=mesh['req'=2,'blk'=16] {'req'}, dimensions={0}, use_global_device_ids=true | all-gather | bytes 1179648 | tf_op jit(solution)/shard_map/all_gather | solution.py:115
  32.7 0.0 copy-done.7
  32.8 0.0 copy-done.9
  32.8 0.4 select_reduce_fusion
  33.2 0.1 copy.33
  33.4 0.0 copy-start.14
  33.4 0.6 iota_compare_fusion
  34.0 0.1 copy.31
  34.2 0.0 copy-start.12
  34.2 1.8 convolution_convert_fusion.4
  36.0 0.8 copy.32
  36.7 0.7 concatenate.47
  37.4 2.6 %fusion.74 = (f32[4,2,128]{2,1,0:T(2,128)S(1)}, f32[4,2,128,384]{2,3,1,0:T(8,128)}) fusion(bf16[128,4,2,96]{0,3,2,1:T(8,128)(2,1)S(1)} %bitcast.134, bf16[256,4,96]{0,2,1:T(8,128)(2,1)S(1)} %bitcast.132, bf16[128,4,48]{0,2,1:T(8,128)(2,1)} %get-tuple-element.16, bf16[128,4,48]{0,2,1:T(8,128)(2,1)} %get-tuple-element.15, pred[384]{0:T(512)(128)(4,1)S(1)} %concatenate.47), kind=kOutput, calls=%fused_computation.93 | convolution fusion | flops 77955456 | bytes 2068864 | tf_op jit(solution)/shard_map/sub | solution.py:78
  40.0 0.0 copy-done.15
  40.1 1.7 convolution_convert_fusion.2
  41.8 0.0 copy-done
  41.8 0.0 copy-start.17
  41.8 0.6 multiply_reduce_fusion.1
  42.4 0.0 copy-start.18
  42.4 0.9 copy-done.3
  43.3 0.0 copy-done.17
  43.3 0.9 multiply_convert_fusion.1
  44.1 0.0 all-gather.2.cloned.1.call-update
  44.2 0.2 reduce-scatter.2.cloned.1.call-start
  44.4 63.3 %all-gather.2.cloned.1.call-done = bf16[2048,1536]{1,0:T(8,128)(2,1)} async-done(((bf16[128,1536]{1,0:T(8,128)(2,1)}), bf16[2048,1536]{1,0:T(8,128)(2,1)}) %all-gather.2.cloned.1.call-update) | async-done | bytes 6291472 | tf_op jit(solution)/shard_map/all_gather | solution.py:86
  107.7 0.0 copy-done.18
  107.7 5.9 %fusion.80 = f32[2048,256]{1,0:T(8,128)} fusion(bf16[2048,1536]{1,0:T(8,128)(2,1)} %all-gather.2.cloned.1.call-done, bf16[1536,256]{1,0:T(8,128)(2,1)S(1)} %copy-done.18), kind=kOutput, calls=%fused_computation.95 | convolution fusion | flops 1610612736 | bytes 9175040 | tf_op jit(solution)/shard_map/dot_general | solution.py:87
  113.6 12.7 %convolution_convert_fusion = bf16[2048,1536]{1,0:T(8,128)(2,1)} fusion(bf16[256,1536]{1,0:T(8,128)(2,1)} %param.27, bf16[2048,1536]{1,0:T(8,128)(2,1)} %all-gather.2.cloned.1.call-done, bf16[1536,256]{1,0:T(8,128)(2,1)} %param.26, f32[2048,256]{1,0:T(8,128)} %fusion.80), kind=kOutput, calls=%fused_computation.2 | convolution fusion | flops 3227516928 | bytes 16252928 | tf_op jit(solution)/shard_map/dot_general | solution.py:91
  126.3 0.0 reduce-scatter.2.cloned.1.call-update
  126.3 0.6 copy-done.19
  126.9 83.3 %reduce-scatter.2.cloned.1.call-done = bf16[128,1536]{1,0:T(8,128)(2,1)} async-done(((bf16[2048,1536]{1,0:T(8,128)(2,1)}), bf16[128,1536]{1,0:T(8,128)(2,1)}) %reduce-scatter.2.cloned.1.call-update) | async-done | bytes 393232 | tf_op jit(solution)/shard_map/reduce_scatter | solution.py:90
  210.2 1.6 multiply_reduce_fusion
  211.9 0.1 multiply_convert_fusion
  212.1 0.2 copy-done.2
  212.3 1.1 fusion.82
  213.3 0.2 copy-done.4
  213.5 0.6 fusion.81
  214.2 0.7 copy-done.6
  214.8 1.0 convolution_convert_fusion.3
  215.8 0.0 copy-done.10
  215.8 0.1 subtract_convert_fusion
  215.9 0.7 subtract_convert_fusion.2
  216.6 1.6 copy.37
  218.2 0.7 pad_maximum_fusion.5
  218.9 2.9 %fusion.77 = (f32[4,2,128]{2,1,0:T(2,128)S(1)}, f32[4,2,128,384]{2,3,1,0:T(8,128)}) fusion(bf16[128,4,2,96]{0,3,2,1:T(8,128)(2,1)} %bitcast.135, bf16[256,4,96]{0,2,1:T(8,128)(2,1)} %bitcast.133, bf16[128,4,48]{0,2,1:T(8,128)(2,1)} %get-tuple-element.14, bf16[128,4,48]{0,2,1:T(8,128)(2,1)} %get-tuple-element.13, pred[384]{0:T(512)(128)(4,1)S(1)} %concatenate.47), kind=kOutput, calls=%fused_computation.94 | convolution fusion | flops 77955456 | bytes 2068864 | tf_op jit(solution)/shard_map/sub | solution.py:78
  221.8 1.8 convolution_convert_fusion.1
  223.5 1.4 fusion.3
  (25 shorter events, 0.1 us)
Async XLA Ops:
  6.5 35.2 %copy-start = (bf16[768,1536]{1,0:T(8,128)(2,1)S(1)}, bf16[768,1536]{1,0:T(8,128)(2,1)}, u32[]{:S(2)}) copy-start(bf16[768,1536]{1,0:T(8,128)(2,1)} %param.23) | copy-start | bytes 7077892
  6.5 101.1 %all-gather.2.cloned.1.call-start = ((), (), s32[]{:S(2)}) async-start(), calls=%async_computation.1 | async-start | bytes 6684672 | tf_op jit(solution)/shard_map/all_gather | solution.py:86
  12.8 2.5 %copy-start.1 = (bf16[1,128,1536]{2,1,0:T(8,128)(2,1)S(1)}, bf16[1,128,1536]{2,1,0:T(8,128)(2,1)}, u32[]{:S(2)}) copy-start(bf16[1,128,1536]{2,1,0:T(8,128)(2,1)} %param.14) | copy-start | bytes 1179652
  12.8 2.5 %copy-start.16 = (f32[1536]{0:T(1024)S(1)}, f32[1536]{0:T(1024)}, u32[]{:S(2)}) copy-start(f32[1536]{0:T(1024)} %param.19) | copy-start | bytes 18436
  15.3 2.6 %copy-start.5 = (bf16[1536,384]{0,1:T(8,128)(2,1)S(1)}, bf16[1536,384]{0,1:T(8,128)(2,1)}, u32[]{:S(2)}) copy-start(bf16[1536,384]{0,1:T(8,128)(2,1)} %copy.34) | copy-start | bytes 3538948
  17.9 1.5 copy-start.11
  18.6 14.1 %copy-start.7 = (f32[128,48]{0,1:T(8,128)}, f32[128,48]{0,1:T(8,128)S(1)}, u32[]{:S(2)}) copy-start(f32[128,48]{0,1:T(8,128)S(1)} %get-tuple-element.17) | copy-start | bytes 73732
  18.6 14.1 %copy-start.9 = (f32[128,48]{0,1:T(8,128)}, f32[128,48]{0,1:T(8,128)S(1)}, u32[]{:S(2)}) copy-start(f32[128,48]{0,1:T(8,128)S(1)} %get-tuple-element.18) | copy-start | bytes 73732
  33.4 6.7 %copy-start.14 = (bf16[1,256,384]{1,2,0:T(8,128)(2,1)}, bf16[1,256,384]{1,2,0:T(8,128)(2,1)S(1)}, u32[]{:S(2)}) copy-start(bf16[1,256,384]{1,2,0:T(8,128)(2,1)S(1)} %copy.33) | copy-start | bytes 589828
  34.2 5.9 %copy-start.12 = (bf16[1,256,384]{1,2,0:T(8,128)(2,1)}, bf16[1,256,384]{1,2,0:T(8,128)(2,1)S(1)}, u32[]{:S(2)}) copy-start(bf16[1,256,384]{1,2,0:T(8,128)(2,1)S(1)} %copy.31) | copy-start | bytes 589828
  37.4 2.7 %copy-start.15 = (bf16[128,384]{0,1:T(8,128)(2,1)S(1)}, bf16[128,384]{0,1:T(8,128)(2,1)}, u32[]{:S(2)}) copy-start(bf16[128,384]{0,1:T(8,128)(2,1)} %copy.32) | copy-start | bytes 294916
  41.8 1.5 copy-start.17
  42.4 0.9 copy-start.3
  42.4 65.3 %copy-start.18 = (bf16[1536,256]{1,0:T(8,128)(2,1)S(1)}, bf16[1536,256]{1,0:T(8,128)(2,1)}, u32[]{:S(2)}) copy-start(bf16[1536,256]{1,0:T(8,128)(2,1)} %param.25) | copy-start | bytes 2359300
  44.2 166.1 %reduce-scatter.2.cloned.1.call-start = ((), (), s32[]{:S(2)}) async-start(), calls=%async_computation.2 | async-start | bytes 6684672 | tf_op jit(solution)/shard_map/reduce_scatter | solution.py:90
  126.3 0.7 copy-start.19
  210.2 2.0 copy-start.2
  212.3 1.3 copy-start.4
  213.5 1.3 copy-start.6
  213.5 2.3 copy-start.8
  213.5 2.3 copy-start.10
  218.9 2.9 %copy-start.13 = (bf16[1,256,384]{1,2,0:T(8,128)(2,1)S(1)}, bf16[1,256,384]{1,2,0:T(8,128)(2,1)}, u32[]{:S(2)}) copy-start(bf16[1,256,384]{1,2,0:T(8,128)(2,1)} %copy-done.12) | copy-start | bytes 589828
Sparse Core Ops, SparseCore 0:
  44.3 63.3 all-gather.1
  126.4 83.7 reduce-scatter.1
where the time goes:
time: 232 us
  waiting for transfers between devices  147 us (63%)
  matrix products  37.1 us (16%)
  between operations  15.1 us (7%)
  local copies, waits for them, and re-layouts  12.7 us (5%)
  blocking collectives  12.7 us (5%)
  other arithmetic  7.21 us (3%)
    reduce_scatter x1, waiting for transfers between devices, run_ffn(): lax.psum_scatter(jnp.dot(hidden_all, w_down, preferred_element_type=jnp.f...  83.3 us
    all_gather x1, waiting for transfers between devices, run_ffn(): part_rows = lax.all_gather(normed_rows, 'blk', axis=0, tiled=True)  63.3 us
    all_gather x1, blocking collectives, local(): part_rows = lax.all_gather(cache_kv, 'req', axis=0, tiled=True)  12.7 us
    dot_general x1, matrix products, run_ffn(): jnp.dot(hidden_all, w_down, preferred_element_type=jnp.float32)  12.7 us
    unnamed x42, local copies, waits for them, and re-layouts  9.37 us
    dot_general x1, matrix products, run_ffn(): gate_vals = jnp.dot(part_rows, w_gate, preferred_element_type=jnp.float32)  5.91 us
    sub x2, matrix products, attend_block(): expd = jnp.exp(scores - peaks)  5.55 us
  transfers between devices with their start and end apart: 2, of which 2 were waited for; matrix products, arithmetic and copies ran while one was open for 0% of the time, Pallas kernels for 0%

commit v1 on v0

v1 whole, which is shorter than its diff:
```python
import functools

import jax
import jax.numpy as jnp
from jax import lax
from jax.experimental import pallas as pl
from jax.experimental.pallas import tpu as pltpu
from jax.sharding import PartitionSpec as P

HEAD = 96
ACCEPT = 64

norm_eps = 1e-05
rope_base = 100000.0


def rms_scale(values, gain_row):
    return (
        values * lax.rsqrt(jnp.mean(values * values, axis=-1, keepdims=True) + norm_eps) * gain_row
    )


def rotate_heads(flat, cosine, sine):
    half_dim = HEAD // 2
    shaped = flat.reshape(flat.shape[0], -1, HEAD)
    cosine, sine = cosine[:, None, :], sine[:, None, :]
    first_half = shaped[..., :half_dim]
    second_half = shaped[..., half_dim:]
    turned = jnp.concatenate(
        [first_half * cosine - second_half * sine, second_half * cosine + first_half * sine],
        axis=-1,
    )
    return turned.reshape(flat.shape)


def attend(queries, all_keys, all_vals, valid, o_weight):
    kv_count = all_keys.shape[1] // HEAD
    rows = queries.shape[0]
    grouped = queries.reshape(rows, kv_count, -1, HEAD)
    keys = all_keys.reshape(-1, kv_count, HEAD)
    vals = all_vals.reshape(-1, kv_count, HEAD)
    scores = jnp.einsum(
        "bgid,kgd->gibk", grouped, keys, preferred_element_type=jnp.float32
    ) * HEAD ** (-0.5)
    scores = jnp.where(valid, scores, -jnp.inf)
    peaks = jnp.max(scores, axis=-1, keepdims=True)
    expd = jnp.exp(scores - peaks)
    probs = (expd / jnp.sum(expd, axis=-1, keepdims=True)).astype(jnp.bfloat16)
    context = jnp.einsum("gibk,kgd->bgid", probs, vals, preferred_element_type=jnp.float32)
    context = context.astype(jnp.bfloat16).reshape(rows, -1)
    return jnp.dot(context, o_weight, preferred_element_type=jnp.float32)


def ffn_kernel(
    A, B, x_ref, wg_ref, wu_ref, wd_ref, out_ref,
    ag, own, core_st, core_land, y_st, y_land, z_st, z_land,
    ag_send, ag_recv, core_send, core_recv, y_send, y_recv, z_send, z_recv,
):
    R = x_ref.shape[0]
    me = lax.axis_index("blk")
    c = lax.rem(me, 2)
    b = lax.rem(me // 2, B)
    a = me // (2 * B)

    def dev(ra, rb, rc):
        na = lax.rem(a + ra, A)
        nb = lax.rem(b + rb, B)
        nc = lax.rem(c + rc, 2)
        return {"blk": (na * B + nb) * 2 + nc}

    peers = [dev(ra, 0, 0) for ra in range(1, A)]
    peers += [dev(0, rb, 0) for rb in range(1, B)]
    peers += [dev(0, 0, 1)]
    barrier = pltpu.get_barrier_semaphore()
    for peer in peers:
        pl.semaphore_signal(barrier, inc=1, device_id=peer, device_id_type=pl.DeviceIdType.MESH)

    started = []

    def send(src, dst, ssem, rsem, to):
        copy = pltpu.make_async_remote_copy(
            src_ref=src, dst_ref=dst, send_sem=ssem, recv_sem=rsem,
            device_id=to, device_id_type=pl.DeviceIdType.MESH,
        )
        copy.start()
        started.append(copy)

    def arrived(dst, rsem):
        pltpu.make_async_copy(dst, dst, rsem).wait()

    def sid(ra, rb, rc):
        return (ra * B + rb) * 2 + rc

    def cid(ra, rb):
        return ra * B + rb

    def ag_slot(ra, rb, rc):
        return ag.at[cid(ra, rb), pl.ds(rc * R, R)]

    n_ag = [0]

    def ag_copy(src, slot, to):
        i = n_ag[0]
        n_ag[0] += 1
        send(ag_slot(*src), ag_slot(*slot), ag_send.at[i], ag_recv.at[sid(*slot)], to)

    def to_core(ra, rb):
        ag_copy((ra, rb, 0), (ra, rb, 1), dev(0, 0, 1))

    def to_y(ra):
        for db in range(1, B):
            ag_copy((ra, 0, 0), (ra, B - db, 0), dev(0, db, 0))

    ag[0, pl.ds(0, R)] = x_ref[...]
    pl.semaphore_wait(barrier, len(peers))

    zorder = sorted(range(1, A), key=lambda r: min(r, A - r))
    to_core(0, 0)
    to_y(0)
    for da in zorder:
        ag_copy((0, 0, 0), (A - da, 0, 0), dev(da, 0, 0))

    order = [(0, 0)] + [(0, rb) for rb in range(1, B)] + [(ra, 0) for ra in zorder]
    order += [(ra, rb) for ra in zorder for rb in range(1, B)]

    def arrive(ra, rb):
        if (ra, rb) == (0, 0):
            return
        arrived(ag_slot(ra, rb, 0), ag_recv.at[sid(ra, rb, 0)])
        if rb == 0:
            to_y(ra)
        to_core(ra, rb)

    def compute(ra, rb):
        i = cid(ra, rb)
        arrived(ag_slot(ra, rb, 1), ag_recv.at[sid(ra, rb, 1)])
        x = ag[i]
        gate = jnp.dot(x, wg_ref[...], preferred_element_type=jnp.float32)
        up = jnp.dot(x, wu_ref[...], preferred_element_type=jnp.float32)
        hidden = (gate / (1.0 + jnp.exp(-gate)) * up).astype(jnp.bfloat16)
        term = jnp.dot(hidden, wd_ref[...], preferred_element_type=jnp.float32)
        term = term.astype(jnp.bfloat16)
        own[i] = term[:R]
        core_st[i] = term[R:]
        send(core_st.at[i], core_land.at[i], core_send.at[i], core_recv.at[i], dev(0, 0, 1))

    def chip_sum(ra, rb):
        i = cid(ra, rb)
        arrived(core_land.at[i], core_recv.at[i])
        return own[i].astype(jnp.float32) + core_land[i].astype(jnp.float32)

    def y_step(ra, rb):
        i = cid(ra, rb)
        j = cid(ra, B - rb)
        y_st[i] = chip_sum(ra, rb).astype(jnp.bfloat16)
        send(y_st.at[i], y_land.at[j], y_send.at[i], y_recv.at[j], dev(0, rb, 0))

    def line_sum(ra):
        total = chip_sum(ra, 0)
        for rb in range(1, B):
            j = cid(ra, rb)
            arrived(y_land.at[j], y_recv.at[j])
            total = total + y_land[j].astype(jnp.float32)
        return total

    def z_step(ra):
        z_st[ra] = line_sum(ra).astype(jnp.bfloat16)
        send(z_st.at[ra], z_land.at[A - ra], z_send.at[ra], z_recv.at[A - ra], dev(ra, 0, 0))

    for k, pair in enumerate(order):
        if 0 < k and k + 1 < len(order):
            arrive(*order[k + 1])
        elif k == 0:
            pass
        compute(*pair)
        if k == 0:
            arrive(*order[1])
        if k >= 1 and order[k - 1][1]:
            y_step(*order[k - 1])
    if order[-1][1]:
        y_step(*order[-1])
    for ra in zorder:
        z_step(ra)
    total = line_sum(0)
    for ra in range(1, A):
        arrived(z_land.at[ra], z_recv.at[ra])
        total = total + z_land[ra].astype(jnp.float32)
    out_ref[...] = total
    for copy in started:
        copy.wait_send()


def run_ffn(x, w_gate, w_up, w_down, count):
    R, D = x.shape
    A = 4
    B = count // (2 * A)
    pairs = A * B
    block = lambda n: pltpu.VMEM((n, R, D), jnp.bfloat16)
    dma = pltpu.SemaphoreType.DMA
    return pl.pallas_call(
        functools.partial(ffn_kernel, A, B),
        out_shape=jax.ShapeDtypeStruct((R, D), jnp.float32),
        in_specs=[pl.BlockSpec(memory_space=pltpu.VMEM)] * 4,
        out_specs=pl.BlockSpec(memory_space=pltpu.VMEM),
        scratch_shapes=[
            pltpu.VMEM((pairs, 2 * R, D), jnp.bfloat16),
            block(pairs), block(pairs), block(pairs), block(pairs), block(pairs),
            block(A), block(A),
            dma((2 * pairs,)), dma((2 * pairs,)),
            dma((pairs,)), dma((pairs,)), dma((pairs,)), dma((pairs,)),
            dma((A,)), dma((A,)),
        ],
        compiler_params=pltpu.CompilerParams(
            collective_id=0, has_side_effects=True, vmem_limit_bytes=56 * 2**20
        ),
    )(x, w_gate, w_up, w_down)


def local(
    count,
    tokens,
    cache_kv,
    cache_len,
    holder,
    accept,
    attn_gain,
    q_weight,
    k_weight,
    v_weight,
    o_weight,
    ffn_gain,
    w_gate,
    w_up,
    w_down,
):
    f32, bf16 = jnp.float32, jnp.bfloat16
    own_holder = holder[0]
    slots = lax.all_gather(cache_kv, "req", axis=0, tiled=True)
    matches = jnp.arange(slots.shape[0], dtype=jnp.int32) == own_holder
    fetched = jnp.sum(
        jnp.where(matches[:, None, None, None], slots, jnp.zeros_like(slots)), axis=0
    )
    cache_keys, cache_vals = fetched[0], fetched[1]
    cache_length = cache_len[0]
    block_rows = tokens[0]
    n = block_rows.shape[0]

    chosen = accept[0] == 1
    at = jnp.arange(n, dtype=jnp.int32)
    before = at[None, :] <= at[:, None]
    count_in = jnp.sum(jnp.where(before & chosen[None, :], 1, 0), axis=1)
    place = jnp.where(chosen, count_in - 1, ACCEPT + at - count_in)
    move = place[None, :] == at[:, None]
    x = jnp.dot(move.astype(bf16), block_rows, preferred_element_type=f32)
    positions = cache_length + jnp.sum(jnp.where(move, at[None, :], 0), axis=1)
    freqs = jnp.exp(
        -jnp.log(rope_base) * 2.0 * jnp.arange(HEAD // 2, dtype=f32) / HEAD
    )
    angles = positions.astype(f32)[:, None] * freqs[None, :]
    cosine, sine = jnp.cos(angles), jnp.sin(angles)
    valid = jnp.concatenate(
        [
            jnp.arange(cache_keys.shape[0], dtype=jnp.int32) < cache_length,
            jnp.ones((n,), dtype=jnp.bool_),
        ]
    )

    def project(rows, weight):
        return jnp.dot(rows, weight, preferred_element_type=f32)

    normed = rms_scale(x, attn_gain).astype(bf16)
    q1 = rotate_heads(project(normed, q_weight), cosine, sine).astype(bf16)
    k1 = rotate_heads(project(normed, k_weight), cosine, sine).astype(bf16)
    v1 = project(normed, v_weight).astype(bf16)
    first = x[:ACCEPT] + attend(
        q1[:ACCEPT],
        jnp.concatenate([cache_keys, k1]),
        jnp.concatenate([cache_vals, v1]),
        valid,
        o_weight,
    )
    ffn = run_ffn(rms_scale(first, ffn_gain).astype(bf16), w_gate, w_up, w_down, count)
    draft = first + ffn
    normed2 = rms_scale(draft, attn_gain).astype(bf16)
    c2, s2 = cosine[:ACCEPT], sine[:ACCEPT]
    q2 = rotate_heads(project(normed2, q_weight), c2, s2).astype(bf16)
    k2 = rotate_heads(project(normed2, k_weight), c2, s2).astype(bf16)
    v2 = project(normed2, v_weight).astype(bf16)
    second = jnp.concatenate([draft, x[ACCEPT:]])
    refined = second + attend(
        jnp.concatenate([q2, q1[ACCEPT:]]),
        jnp.concatenate([cache_keys, k2, k1[ACCEPT:]]),
        jnp.concatenate([cache_vals, v2, v1[ACCEPT:]]),
        valid,
        o_weight,
    )
    back = (place[:, None] == at[None, :]).astype(f32)
    return jnp.dot(back, refined, precision=lax.Precision.HIGHEST)[None]


def solution(mesh):
    return jax.shard_map(
        functools.partial(local, mesh.shape["blk"]),
        mesh=mesh,
        in_specs=(
            P(("req", "blk"), None, None),
            P(("req", "blk"), None, None, None),
            P(("req", "blk")),
            P(("req", "blk")),
            P(("req", "blk"), None),
            P(),
            P(),
            P(),
            P(),
            P(),
            P(),
            P(None, "blk"),
            P(None, "blk"),
            P("blk", None),
        ),
        out_specs=P(("req", "blk"), None, None),
        check_vma=False,
    )
```

time: 232 us -> 120 us (0.52)
  waiting for transfers between devices: 147 us -> 0 us
  Pallas kernels: 0 us -> 58.5 us
  between operations: 15.1 us -> 1.92 us
  matrix products: 37.1 us -> 24.7 us
    reduce_scatter x1 -> x0, waiting for transfers between devices: 83.3 us -> none  [run_ffn(): lax.psum_scatter(jnp.dot(hidden_all, w_down, preferred_element_type=jnp.f...]
    all_gather x1 -> x0, waiting for transfers between devices: 63.3 us -> none  [run_ffn(): part_rows = lax.all_gather(normed_rows, 'blk', axis=0, tiled=True)]
    pallas_call x0 -> x1, Pallas kernels: none -> 58.5 us  [run_ffn(): pl.pallas_call(functools.partial(ffn_kernel, A, B), out_shape=jax.ShapeDt...]
    dot_general x12 -> x13, matrix products: 31.6 us -> 20.7 us  [the longest x6 10.7 us: project(): return jnp.dot(rows, weight, preferred_element_type=f32)]
    unnamed x42 -> x54, local copies, waits for them, and re-layouts: 9.37 us -> 2.07 us
    slice x3 -> x8, local copies, waits for them, and re-layouts: 0.33 us -> 5.21 us  [the longest x3 1.7 us: local(): cache_keys, cache_vals = (fetched[0], fetched[1])]
  transfers between devices with their start and end apart: 2 -> 0, of which waited for: 2 -> 0; matrix products, arithmetic and copies ran while one was open for 0% -> 0% of each run, Pallas kernels for 0% -> 0%
where the time goes in v1:
time: 120 us; the launch traced here: 119 us
  Pallas kernels  58.5 us (49%)
  matrix products  24.7 us (21%)
  local copies, waits for them, and re-layouts  13.7 us (11%)
  blocking collectives  13 us (11%)
  other arithmetic  7.17 us (6%)
  between operations  1.92 us (2%)
    pallas_call x1, Pallas kernels, run_ffn(): pl.pallas_call(functools.partial(ffn_kernel, A, B), out_shape=jax.ShapeDt...  58.5 us
    all_gather x1, blocking collectives, local(): slots = lax.all_gather(cache_kv, 'req', axis=0, tiled=True)  13 us
    dot_general x6, matrix products, project(): return jnp.dot(rows, weight, preferred_element_type=f32)  10.7 us
    dot_general x2, matrix products, attend(): jnp.einsum('gibk,kgd->bgid', probs, vals, preferred_element_type=jnp.floa...  4.28 us
    sub x2, matrix products, attend(): expd = jnp.exp(scores - peaks)  3.94 us

profile of v1, /device:TPU:0, one launch (start us, length us, event | category | flops | bytes accessed | tf_op | source)
XLA Modules:
  0.0 118.9 jit_solution(14605112872188467936)
XLA Ops:
  1.5 0.7 compare_bitcast_fusion
  2.1 0.1 select_reduce_fusion.2
  2.2 0.7 fusion.41
  2.9 0.7 subtract_select_fusion
  3.6 0.1 select_reduce_fusion.1
  3.7 0.2 multiply_cosine_fusion
  3.9 0.7 copy.66
  4.6 0.7 copy.65
  5.3 13.0 %all_gather.3 = bf16[2,2,256,384]{3,2,1,0:T(8,128)(2,1)S(1)} all-gather(bf16[1,2,256,384]{3,2,1,0:T(8,128)(2,1)} %param.15), channel_id=1, replica_groups=mesh['req'=2,'blk'=16] {'req'}, dimensions={0}, use_global_device_ids=true | all-gather | bytes 1179648 | tf_op jit(solution)/shard_map/all_gather | solution.py:238
  18.3 0.4 select_reduce_fusion
  18.7 0.0 copy-start.24
  18.8 0.8 copy.55
  19.6 0.8 copy.57
  20.4 1.0 multiply_reduce_fusion
  21.4 0.1 multiply_convert_fusion
  21.6 1.6 %convolution_convert_fusion.2 = bf16[128,384]{1,0:T(8,128)(2,1)S(1)} fusion(bf16[128,1536]{1,0:T(8,128)(2,1)S(1)} %multiply_convert_fusion, bf16[1536,384]{1,0:T(8,128)(2,1)} %param.22), kind=kOutput, calls=%fused_computation.18 | convolution fusion | flops 151044096 | bytes 1671168 | tf_op jit(solution)/shard_map/dot_general | solution.py:269
  23.2 0.0 copy-start.11
  23.2 0.6 copy-done.11
  23.9 0.6 slice.88
  24.5 1.6 %copy.56 = bf16[128,384]{0,1:T(8,128)(2,1)} copy(bf16[128,384]{1,0:T(8,128)(2,1)} %copy-done.11) | data formatting | bytes 196608 | tf_op jit(solution)/shard_map/convert_element_type | solution.py:274
  26.1 1.5 %copy.77 = bf16[64,384]{0,1:T(8,128)(2,1)} copy(bf16[64,384]{1,0:T(8,128)(2,1)} %slice.88) | data formatting | bytes 98304 | tf_op jit(solution)/shard_map/concatenate | solution.py:293
  27.7 1.9 %fusion.64 = f32[128,384]{0,1:T(8,128)S(1)} fusion(bf16[128,1536]{1,0:T(8,128)(2,1)S(1)} %multiply_convert_fusion, bf16[1536,384]{1,0:T(8,128)(2,1)} %param.21), kind=kOutput, calls=%fused_computation.99 | convolution fusion | flops 150994944 | bytes 1769472 | tf_op jit(solution)/shard_map/dot_general | solution.py:269
  29.6 2.7 %fusion.65 = f32[128,768]{0,1:T(8,128)S(1)} fusion(bf16[128,1536]{1,0:T(8,128)(2,1)S(1)} %multiply_convert_fusion, bf16[1536,768]{1,0:T(8,128)(2,1)} %param.20), kind=kOutput, calls=%fused_computation.100 | convolution fusion | flops 301989888 | bytes 3145728 | tf_op jit(solution)/shard_map/dot_general | solution.py:269
  32.3 0.0 copy-start.8
  32.3 0.0 copy-done.13
  32.3 0.0 copy-done.16
  32.3 0.1 subtract_convert_fusion.1
  32.4 0.7 slice.93
  33.1 0.8 slice_maximum_fusion
  34.0 0.0 copy-done.8
  34.0 2.0 %fusion.58 = f32[4,2,64]{2,1,0:T(2,128)} fusion(bf16[64,4,2,96]{0,3,2,1:T(8,128)(2,1)} %bitcast.117, pred[384]{0:T(512)(128)(4,1)S(1)} %concatenate.53, bf16[256,4,96]{0,2,1:T(8,128)(2,1)S(1)} %bitcast.113, bf16[128,4,96]{0,2,1:T(8,128)(2,1)S(1)} %maximum_convert_fusion), kind=kOutput, calls=%fused_computation.97 | convolution fusion | flops 39125376 | bytes 395648 | tf_op jit(solution)/shard_map/sub | solution.py:47
  36.0 0.8 slice.87
  36.8 2.1 %fusion.10 = f32[4,2,64,384]{3,2,1,0:T(8,128)} fusion(bf16[64,4,2,96]{0,3,2,1:T(8,128)(2,1)} %bitcast.118, pred[384]{0:T(512)(128)(4,1)S(1)} %concatenate.53, bf16[256,4,96]{0,2,1:T(8,128)(2,1)S(1)} %bitcast.114, bf16[128,4,96]{0,2,1:T(8,128)(2,1)S(1)} %maximum_convert_fusion), kind=kOutput, calls=%fused_computation.15 | convolution fusion | flops 38731776 | bytes 1180032 | tf_op jit(solution)/shard_map/bgid,kgd->gibk/dot_general | solution.py:42
  38.9 2.5 %fusion.11 = bf16[64,4,2,96]{3,0,2,1:T(8,128)(2,1)S(1)} fusion(f32[4,2,64]{2,1,0:T(2,128)} %fusion.58, bf16[256,4,96]{0,2,1:T(8,128)(2,1)} %bitcast.127, bf16[128,4,96]{0,2,1:T(8,128)(2,1)S(1)} %bitcast.132, f32[4,2,64,384]{3,2,1,0:T(8,128)} %fusion.10), kind=kOutput, calls=%fused_computation.19 | convolution fusion | flops 38978432 | bytes 1181696 | tf_op jit(solution)/shard_map/gibk,kgd->bgid/dot_general | solution.py:49
  41.4 0.2 copy.61
  41.6 0.1 reshape.185
  41.7 0.0 copy-start.25
  41.7 0.6 multiply_reduce_fusion.2
  42.4 0.0 copy-done.25
  42.4 0.8 multiply_convert_fusion.2.x_ref
  43.2 58.5 %shard_map.136 = f32[64,1536]{1,0:T(8,128)} custom-call(bf16[64,1536]{1,0:T(8,128)(2,1)} %multiply_convert_fusion.2.x_ref, bf16[1536,256]{1,0:T(8,128)(2,1)} %wg_ref.1, bf16[1536,256]{1,0:T(8,128)(2,1)} %wu_ref.1, bf16[256,1536]{1,0:T(8,128)(2,1)} %wd_ref.1), custom_call_target="tpu_custom_call" | custom-call | tf_op jit(solution)/shard_map/pallas_call | solution.py:200
  101.7 0.0 copy-start.1
  101.7 1.2 %multiply_reduce_fusion.1 = (f32[64]{0:T(128)S(1)}, f32[64,1536]{1,0:T(8,128)S(1)}) fusion(f32[64,1536]{1,0:T(8,128)S(1)} %get-tuple-element.24, f32[64,1536]{1,0:T(8,128)} %shard_map.136), kind=kLoop, calls=%fused_computation.28 | loop fusion | flops 294848 | bytes 1179904 | tf_op jit(solution)/shard_map/reduce_sum | solution.py:19
  102.9 0.0 copy-start.3
  102.9 0.1 multiply_convert_fusion.1
  103.1 0.6 copy-done.3
  103.7 0.7 copy-done.5
  104.4 0.9 convolution_convert_fusion.3
  105.3 1.6 %copy.62 = bf16[64,384]{0,1:T(8,128)(2,1)} copy(bf16[64,384]{1,0:T(8,128)(2,1)} %convolution_convert_fusion.3) | data formatting | bytes 98304 | tf_op jit(solution)/shard_map/convert_element_type | solution.py:288
  106.9 3.0 %fusion.67 = f32[64,768]{1,0:T(8,128)} fusion(bf16[64,1536]{1,0:T(8,128)(2,1)} %copy-done.5, bf16[1536,768]{1,0:T(8,128)(2,1)} %param.20), kind=kOutput, calls=%fused_computation.102 | convolution fusion | flops 150994944 | bytes 2752512 | tf_op jit(solution)/shard_map/dot_general | solution.py:269
  110.0 0.6 fusion.66
  110.6 1.2 reshape.187
  111.8 0.9 subtract_convert_fusion
  112.7 0.1 pad_maximum_fusion.6
  112.9 0.2 copy.78
  113.0 0.0 copy-done.10
  113.0 0.1 pad_maximum_fusion.5
  113.2 0.0 copy-done.9
  113.2 0.0 copy-done.21
  113.2 1.9 %fusion.61 = (f32[4,2,128]{2,1,0:T(2,128)S(1)}, f32[4,2,128,384]{2,3,1,0:T(8,128)}) fusion(bf16[128,4,2,96]{0,3,2,1:T(8,128)(2,1)S(1)} %bitcast.129, bf16[256,4,96]{0,2,1:T(8,128)(2,1)S(1)} %bitcast.115, bf16[64,4,96]{0,2,1:T(8,128)(2,1)S(1)} %copy-done.21, bf16[64,4,48]{0,2,1:T(8,128)(2,1)S(1)} %get-tuple-element.14, ...), kind=kOutput, calls=%fused_computation.98 | convolution fusion | flops 78250368 | bytes 2068864 | tf_op jit(solution)/shard_map/sub | solution.py:47
  115.1 0.0 copy-start.4
  115.2 1.8 %convolution_convert_fusion = bf16[4,96,2,128]{3,1,2,0:T(8,128)(2,1)S(1)} fusion(f32[4,2,128,384]{2,3,1,0:T(8,128)} %get-tuple-element.26, f32[4,2,128]{2,1,0:T(2,128)S(1)} %get-tuple-element.25, bf16[256,4,96]{0,2,1:T(8,128)(2,1)S(1)} %bitcast.128, bf16[64,4,96]{0,2,1:T(8,128)(2,1)S(1)} %bitcast.130, bf16[64,4,96]{0,2,1:T(8,128)(2,1)S(1)} %bitcast.131), kind=kOutput, calls=%fused_computation.16 | convolution fusion | flops 77266944 | bytes 2068480 | tf_op jit(solution)/shard_map/gibk,kgd->bgid/dot_general | solution.py:49
  117.0 0.5 convolution_add_fusion
  117.5 1.4 %convolution_bitcast_fusion = f32[1,128,1536]{2,1,0:T(8,128)} fusion(f32[128,1536]{1,0:T(8,128)S(1)} %convolution_add_fusion, s32[128]{0:T(128)S(1)} %subtract_select_fusion), kind=kOutput, calls=%fused_computation.3 | convolution fusion | flops 302006272 | bytes 1573376 | tf_op jit(solution)/shard_map/dot_general | solution.py:298
  (49 shorter events, 0.2 us)
Async XLA Ops:
  0.0 41.7 %copy-start = (bf16[768,1536]{1,0:T(8,128)(2,1)S(1)}, bf16[768,1536]{1,0:T(8,128)(2,1)}, u32[]{:S(2)}) copy-start(bf16[768,1536]{1,0:T(8,128)(2,1)} %param.23) | copy-start | bytes 7077892
  2.9 0.8 copy-start.26
  3.9 14.4 %copy-start.12 = (f32[128,48]{0,1:T(8,128)}, f32[128,48]{0,1:T(8,128)S(1)}, u32[]{:S(2)}) copy-start(f32[128,48]{0,1:T(8,128)S(1)} %get-tuple-element.19) | copy-start | bytes 73732
  3.9 14.4 %copy-start.15 = (f32[128,48]{0,1:T(8,128)}, f32[128,48]{0,1:T(8,128)S(1)}, u32[]{:S(2)}) copy-start(f32[128,48]{0,1:T(8,128)S(1)} %get-tuple-element.20) | copy-start | bytes 73732
  18.3 2.1 %copy-start.18 = (bf16[1,128,1536]{2,1,0:T(8,128)(2,1)S(1)}, bf16[1,128,1536]{2,1,0:T(8,128)(2,1)}, u32[]{:S(2)}) copy-start(bf16[1,128,1536]{2,1,0:T(8,128)(2,1)} %param.14) | copy-start | bytes 1179652
  18.7 2.7 %copy-start.24 = (f32[1536]{0:T(1024)S(1)}, f32[1536]{0:T(1024)}, u32[]{:S(2)}) copy-start(f32[1536]{0:T(1024)} %param.19) | copy-start | bytes 18436
  23.2 0.6 copy-start.11
  29.5 2.7 %copy-start.13 = (f32[128,48]{0,1:T(8,128)S(1)}, f32[128,48]{0,1:T(8,128)}, u32[]{:S(2)}) copy-start(f32[128,48]{0,1:T(8,128)} %copy-done.12) | copy-start | bytes 73732
  29.5 2.7 %copy-start.16 = (f32[128,48]{0,1:T(8,128)S(1)}, f32[128,48]{0,1:T(8,128)}, u32[]{:S(2)}) copy-start(f32[128,48]{0,1:T(8,128)} %copy-done.15) | copy-start | bytes 73732
  32.3 1.7 %copy-start.8 = (bf16[1,256,384]{1,2,0:T(8,128)(2,1)S(1)}, bf16[1,256,384]{1,2,0:T(8,128)(2,1)}, u32[]{:S(2)}) copy-start(bf16[1,256,384]{1,2,0:T(8,128)(2,1)} %copy.57) | copy-start | bytes 589828
  34.0 4.9 %copy-start.23 = (bf16[128,384]{0,1:T(8,128)(2,1)S(1)}, bf16[128,384]{0,1:T(8,128)(2,1)}, u32[]{:S(2)}) copy-start(bf16[128,384]{0,1:T(8,128)(2,1)} %copy.56) | copy-start | bytes 294916
  41.7 0.7 copy-start.25
  101.7 2.7 %copy-start.1 = (bf16[1536,384]{1,0:T(8,128)(2,1)S(1)}, bf16[1536,384]{1,0:T(8,128)(2,1)}, u32[]{:S(2)}) copy-start(bf16[1536,384]{1,0:T(8,128)(2,1)} %param.22) | copy-start | bytes 3538948
  102.9 0.8 copy-start.3
  103.7 0.7 copy-start.5
  105.3 4.7 %copy-start.2 = (bf16[1536,384]{1,0:T(8,128)(2,1)S(1)}, bf16[1536,384]{1,0:T(8,128)(2,1)}, u32[]{:S(2)}) copy-start(bf16[1536,384]{1,0:T(8,128)(2,1)} %param.21) | copy-start | bytes 3538948
  106.9 3.0 %copy-start.6 = (bf16[64,1536]{1,0:T(8,128)(2,1)S(1)}, bf16[64,1536]{1,0:T(8,128)(2,1)}, u32[]{:S(2)}) copy-start(bf16[64,1536]{1,0:T(8,128)(2,1)} %copy-done.5) | copy-start | bytes 589828
  106.9 3.7 %copy-start.14 = (f32[128,48]{0,1:T(8,128)S(1)}, f32[128,48]{0,1:T(8,128)}, u32[]{:S(2)}) copy-start(f32[128,48]{0,1:T(8,128)} %copy-done.12) | copy-start | bytes 73732
  106.9 3.7 %copy-start.17 = (f32[128,48]{0,1:T(8,128)S(1)}, f32[128,48]{0,1:T(8,128)}, u32[]{:S(2)}) copy-start(f32[128,48]{0,1:T(8,128)} %copy-done.15) | copy-start | bytes 73732
  110.5 2.5 %copy-start.10 = (bf16[64,8,96]{0,2,1:T(8,128)(2,1)S(1)}, bf16[64,8,96]{0,2,1:T(8,128)(2,1)}, u32[]{:S(2)}) copy-start(bf16[64,8,96]{0,2,1:T(8,128)(2,1)} %get-tuple-element.18) | copy-start | bytes 294916
  110.6 2.6 %copy-start.9 = (bf16[1,256,384]{1,2,0:T(8,128)(2,1)S(1)}, bf16[1,256,384]{1,2,0:T(8,128)(2,1)}, u32[]{:S(2)}) copy-start(bf16[1,256,384]{1,2,0:T(8,128)(2,1)} %copy.57) | copy-start | bytes 589828
  110.6 2.6 %copy-start.21 = (bf16[64,4,96]{0,2,1:T(8,128)(2,1)S(1)}, bf16[64,4,96]{0,2,1:T(8,128)(2,1)}, u32[]{:S(2)}) copy-start(bf16[64,4,96]{0,2,1:T(8,128)(2,1)} %slice.93) | copy-start | bytes 147460
  113.2 1.9 %copy-start.19 = (bf16[1,256,384]{1,2,0:T(8,128)(2,1)S(1)}, bf16[1,256,384]{1,2,0:T(8,128)(2,1)}, u32[]{:S(2)}) copy-start(bf16[1,256,384]{1,2,0:T(8,128)(2,1)} %copy.55) | copy-start | bytes 589828
  113.2 1.9 %copy-start.20 = (bf16[64,384]{0,1:T(8,128)(2,1)S(1)}, bf16[64,384]{0,1:T(8,128)(2,1)}, u32[]{:S(2)}) copy-start(bf16[64,384]{0,1:T(8,128)(2,1)} %copy.77) | copy-start | bytes 147460
  113.2 1.9 %copy-start.22 = (bf16[64,384]{0,1:T(8,128)(2,1)S(1)}, bf16[64,384]{0,1:T(8,128)(2,1)}, u32[]{:S(2)}) copy-start(bf16[64,384]{0,1:T(8,128)(2,1)} %copy.62) | copy-start | bytes 147460
  115.1 1.8 %copy-start.4 = (f32[64,1536]{1,0:T(8,128)S(1)}, f32[64,1536]{1,0:T(8,128)}, u32[]{:S(2)}) copy-start(f32[64,1536]{1,0:T(8,128)} %copy-done.3) | copy-start | bytes 1179652
  115.2 1.8 %copy-start.7 = (f32[64,1536]{1,0:T(8,128)S(1)}, f32[64,1536]{1,0:T(8,128)}, u32[]{:S(2)}) copy-start(f32[64,1536]{1,0:T(8,128)} %slice.87) | copy-start | bytes 1179652

commit v2 on v1

v2 whole, which is shorter than its diff:
```python
import functools

import jax
import jax.numpy as jnp
from jax import lax
from jax.experimental import pallas as pl
from jax.experimental.pallas import tpu as pltpu
from jax.sharding import PartitionSpec as P

HEAD = 96
ACCEPT = 64

norm_eps = 1e-05
rope_base = 100000.0


def rms_scale(values, gain_row):
    return (
        values * lax.rsqrt(jnp.mean(values * values, axis=-1, keepdims=True) + norm_eps) * gain_row
    )


def dot(x, y):
    return jnp.dot(x, y, preferred_element_type=jnp.float32)


def pick(mask, values):
    high = values.astype(jnp.bfloat16)
    rest = values - high.astype(jnp.float32)
    mid = rest.astype(jnp.bfloat16)
    low = (rest - mid.astype(jnp.float32)).astype(jnp.bfloat16)
    return dot(mask, high) + dot(mask, mid) + dot(mask, low)


def rotate(flat, cosine, sine):
    width = flat.shape[1]
    half = HEAD // 2
    lane = lax.broadcasted_iota(jnp.int32, flat.shape, 1)
    ahead = pltpu.roll(flat, width - half, 1)
    behind = pltpu.roll(flat, half, 1)
    other = jnp.where(lane % HEAD < half, ahead, behind)
    return (flat * cosine + other * sine).astype(jnp.bfloat16)


def attend(q, kc, vc, kn, vn, length):
    rows = q.shape[0]
    kv_count = kc.shape[1] // HEAD
    group = q.shape[1] // HEAD // kv_count
    nt = (((1,), (1,)), ((), ()))
    outs = []
    for g in range(kv_count):
        cols = slice(g * HEAD, (g + 1) * HEAD)
        qs = jnp.concatenate(
            [q[:, (g * group + i) * HEAD : (g * group + i + 1) * HEAD] for i in range(group)]
        )
        sc = lax.dot_general(qs, kc[:, cols], nt, preferred_element_type=jnp.float32)
        sn = lax.dot_general(qs, kn[:, cols], nt, preferred_element_type=jnp.float32)
        lane = lax.broadcasted_iota(jnp.int32, sc.shape, 1)
        sc = jnp.where(lane < length, sc * HEAD ** (-0.5), -jnp.inf)
        sn = sn * HEAD ** (-0.5)
        peak = jnp.maximum(
            jnp.max(sc, axis=-1, keepdims=True), jnp.max(sn, axis=-1, keepdims=True)
        )
        ec, en = jnp.exp(sc - peak), jnp.exp(sn - peak)
        total = jnp.sum(ec, axis=-1, keepdims=True) + jnp.sum(en, axis=-1, keepdims=True)
        scale = 1.0 / total
        pc, pn = (ec * scale).astype(jnp.bfloat16), (en * scale).astype(jnp.bfloat16)
        ctx = dot(pc, vc[:, cols]) + dot(pn, vn[:, cols])
        outs += [ctx[i * rows : (i + 1) * rows] for i in range(group)]
    return jnp.concatenate(outs, axis=1).astype(jnp.bfloat16)


def layer_kernel(
    A, B, G, length_ref, holder_ref, accept_ref, tokens_ref, cos_ref, sin_ref, again_ref, fgain_ref,
    cache_hbm, wq_hbm, wk_hbm, wv_hbm, wo_hbm, wg_hbm, wu_hbm, wd_hbm, out_ref,
    wq_ref, wk_ref, wv_ref, wo_ref, wg_ref, wu_ref, wd_ref, slots, kc_ref, vc_ref,
    q_ref, kn_ref, vn_ref, x_ref, cosp, sinp, load_sem, slot_send, slot_recv,
    ag, own, core_st, core_land, y_st, y_land, z_st, z_land,
    ag_send, ag_recv, core_send, core_recv, y_send, y_recv, z_send, z_recv,
):
    R = ACCEPT
    f32, bf16 = jnp.float32, jnp.bfloat16
    n = tokens_ref.shape[0]
    loads = [
        pltpu.make_async_copy(s, d, load_sem.at[i])
        for i, (s, d) in enumerate(
            [(wq_hbm, wq_ref), (wk_hbm, wk_ref), (wv_hbm, wv_ref), (cache_hbm, slots.at[0]),
             (wo_hbm, wo_ref), (wg_hbm, wg_ref), (wu_hbm, wu_ref), (wd_hbm, wd_ref)]
        )
    ]
    for load in loads:
        load.start()
    req = lax.axis_index("req")
    me = lax.axis_index("blk")
    c = lax.rem(me, 2)
    b = lax.rem(me // 2, B)
    a = me // (2 * B)

    def dev(ra, rb, rc):
        na = lax.rem(a + ra, A)
        nb = lax.rem(b + rb, B)
        nc = lax.rem(c + rc, 2)
        return {"blk": (na * B + nb) * 2 + nc}

    def column(r):
        return {"req": lax.rem(req + r, G)}

    peers = [dev(ra, 0, 0) for ra in range(1, A)]
    peers += [dev(0, rb, 0) for rb in range(1, B)]
    peers += [dev(0, 0, 1)]
    peers += [column(r) for r in range(1, G)]
    barrier = pltpu.get_barrier_semaphore()
    for peer in peers:
        pl.semaphore_signal(barrier, inc=1, device_id=peer, device_id_type=pl.DeviceIdType.MESH)

    started = []

    def send(src, dst, ssem, rsem, to):
        copy = pltpu.make_async_remote_copy(
            src_ref=src, dst_ref=dst, send_sem=ssem, recv_sem=rsem,
            device_id=to, device_id_type=pl.DeviceIdType.MESH,
        )
        copy.start()
        started.append(copy)

    def arrived(dst, rsem):
        pltpu.make_async_copy(dst, dst, rsem).wait()

    def sid(ra, rb, rc):
        return (ra * B + rb) * 2 + rc

    def cid(ra, rb):
        return ra * B + rb

    def ag_slot(ra, rb, rc):
        return ag.at[cid(ra, rb), pl.ds(rc * R, R)]

    n_ag = [0]

    def ag_copy(src, slot, to):
        i = n_ag[0]
        n_ag[0] += 1
        send(ag_slot(*src), ag_slot(*slot), ag_send.at[i], ag_recv.at[sid(*slot)], to)

    def to_core(ra, rb):
        ag_copy((ra, rb, 0), (ra, rb, 1), dev(0, 0, 1))

    def to_y(ra):
        for db in range(1, B):
            ag_copy((ra, 0, 0), (ra, B - db, 0), dev(0, db, 0))

    pl.semaphore_wait(barrier, len(peers))
    for r in range(1, G):
        send(cache_hbm, slots.at[G - r], slot_send.at[r], slot_recv.at[G - r], column(r))

    chosen = accept_ref[...] == 1
    row = lax.broadcasted_iota(jnp.int32, (n, n), 0)
    col = lax.broadcasted_iota(jnp.int32, (n, n), 1)
    tri = jnp.where(row <= col, 1.0, 0.0).astype(bf16)
    taken = jnp.broadcast_to(jnp.where(chosen, 1.0, 0.0), (16, n)).astype(bf16)
    upto = dot(taken, tri)[:1].astype(jnp.int32)
    at = lax.broadcasted_iota(jnp.int32, (1, n), 1)
    place = jnp.where(chosen, upto - 1, R + at - upto)
    move32 = jnp.where(row == place, 1.0, 0.0)
    move = move32.astype(bf16)
    x_ref[...] = dot(move, tokens_ref[...])
    cosp[...] = pick(move, cos_ref[...])
    sinp[...] = pick(move, sin_ref[...])
    length = length_ref[0]
    kw = kn_ref.shape[1]

    normed = rms_scale(x_ref[...], again_ref[...]).astype(bf16)
    loads[0].wait()
    q_ref[...] = rotate(dot(normed, wq_ref[...]), cosp[...], sinp[...])
    loads[1].wait()
    kn_ref[...] = rotate(dot(normed, wk_ref[...]), cosp[:, :kw], sinp[:, :kw])
    loads[2].wait()
    vn_ref[...] = dot(normed, wv_ref[...]).astype(bf16)

    loads[3].wait()
    kc, vc = slots[0, 0], slots[0, 1]
    for r in range(1, G):
        arrived(slots.at[r], slot_recv.at[r])
        here = lax.rem(req + r, G) == holder_ref[0]
        kc = jnp.where(here, slots[r, 0], kc)
        vc = jnp.where(here, slots[r, 1], vc)
    kc_ref[...] = kc
    vc_ref[...] = vc

    ctx = attend(q_ref[:R], kc_ref[...], vc_ref[...], kn_ref[...], vn_ref[...], length)
    loads[4].wait()
    first = x_ref[:R] + dot(ctx, wo_ref[...])
    x_ref[:R] = first
    ag[0, pl.ds(0, R)] = rms_scale(first, fgain_ref[...]).astype(bf16)

    up_steps = A // 2
    down_steps = A - 1 - up_steps
    zorder = []
    for k in range(1, up_steps + 1):
        zorder.append(A - k)
        if k <= down_steps:
            zorder.append(k)

    def to_z(ra):
        k = (A - ra) % A
        if k < up_steps and (ra == 0 or ra > down_steps):
            ag_copy((ra, 0, 0), ((ra - 1) % A, 0, 0), dev(1, 0, 0))
        if ra < down_steps:
            ag_copy((ra, 0, 0), (ra + 1, 0, 0), dev(A - 1, 0, 0))

    to_z(0)
    to_y(0)
    to_core(0, 0)
    for load in loads[5:]:
        load.wait()

    order = [(0, 0)] + [(0, rb) for rb in range(1, B)] + [(ra, 0) for ra in zorder]
    order += [(ra, rb) for ra in zorder for rb in range(1, B)]

    def arrive(ra, rb):
        if (ra, rb) == (0, 0):
            return
        arrived(ag_slot(ra, rb, 0), ag_recv.at[sid(ra, rb, 0)])
        if rb == 0:
            to_z(ra)
            to_y(ra)
        to_core(ra, rb)

    def compute(ra, rb):
        i = cid(ra, rb)
        arrived(ag_slot(ra, rb, 1), ag_recv.at[sid(ra, rb, 1)])
        x = ag[i]
        gate = jnp.dot(x, wg_ref[...], preferred_element_type=jnp.float32)
        up = jnp.dot(x, wu_ref[...], preferred_element_type=jnp.float32)
        hidden = (gate / (1.0 + jnp.exp(-gate)) * up).astype(jnp.bfloat16)
        term = jnp.dot(hidden, wd_ref[...], preferred_element_type=jnp.float32)
        term = term.astype(jnp.bfloat16)
        own[i] = term[:R]
        core_st[i] = term[R:]
        send(core_st.at[i], core_land.at[i], core_send.at[i], core_recv.at[i], dev(0, 0, 1))

    def chip_sum(ra, rb):
        i = cid(ra, rb)
        arrived(core_land.at[i], core_recv.at[i])
        return own[i].astype(jnp.float32) + core_land[i].astype(jnp.float32)

    def y_step(ra, rb):
        i = cid(ra, rb)
        j = cid(ra, B - rb)
        y_st[i] = chip_sum(ra, rb).astype(jnp.bfloat16)
        send(y_st.at[i], y_land.at[j], y_send.at[i], y_recv.at[j], dev(0, rb, 0))

    def line_sum(ra):
        total = chip_sum(ra, 0)
        for rb in range(1, B):
            j = cid(ra, rb)
            arrived(y_land.at[j], y_recv.at[j])
            total = total + y_land[j].astype(jnp.float32)
        return total

    def z_step(ra):
        z_st[ra] = line_sum(ra).astype(jnp.bfloat16)
        send(z_st.at[ra], z_land.at[A - ra], z_send.at[ra], z_recv.at[A - ra], dev(ra, 0, 0))

    for k, pair in enumerate(order):
        if 0 < k and k + 1 < len(order):
            arrive(*order[k + 1])
        elif k == 0:
            pass
        compute(*pair)
        if k == 0:
            arrive(*order[1])
        if k >= 1 and order[k - 1][1]:
            y_step(*order[k - 1])
    if order[-1][1]:
        y_step(*order[-1])
    for ra in zorder:
        z_step(ra)
    total = line_sum(0)
    for ra in range(1, A):
        arrived(z_land.at[ra], z_recv.at[ra])
        total = total + z_land[ra].astype(jnp.float32)
    draft = x_ref[:R] + total
    x_ref[:R] = draft
    normed = rms_scale(draft, again_ref[...]).astype(bf16)
    q_ref[:R] = rotate(dot(normed, wq_ref[...]), cosp[:R], sinp[:R])
    kn_ref[:R] = rotate(dot(normed, wk_ref[...]), cosp[:R, :kw], sinp[:R, :kw])
    vn_ref[:R] = dot(normed, wv_ref[...]).astype(bf16)
    ctx = attend(q_ref[...], kc_ref[...], vc_ref[...], kn_ref[...], vn_ref[...], length)
    refined = x_ref[...] + dot(ctx, wo_ref[...])
    out_ref[...] = pick(move32.T.astype(bf16), refined)
    for copy in started:
        copy.wait_send()


def local(
    mesh_shape,
    tokens,
    cache_kv,
    cache_len,
    holder,
    accept,
    attn_gain,
    q_weight,
    k_weight,
    v_weight,
    o_weight,
    ffn_gain,
    w_gate,
    w_up,
    w_down,
):
    f32, bf16 = jnp.float32, jnp.bfloat16
    n, D = tokens.shape[1:]
    qw, kw = q_weight.shape[1], k_weight.shape[1]
    cs = cache_kv.shape[2]
    positions = (cache_len[0] + jnp.arange(n, dtype=jnp.int32)).astype(f32)
    lane = jnp.arange(qw, dtype=jnp.int32) % HEAD
    half = HEAD // 2
    freqs = jnp.exp(-jnp.log(rope_base) * 2.0 * (lane % half).astype(f32) / HEAD)
    angles = positions[:, None] * freqs[None, :]
    cosine = jnp.cos(angles)
    sine = jnp.where(lane < half, -1.0, 1.0) * jnp.sin(angles)
    R = ACCEPT
    A = 4
    B = mesh_shape["blk"] // (2 * A)
    G = mesh_shape["req"]
    pairs = A * B
    block = lambda m: pltpu.VMEM((m, R, D), bf16)
    dma = pltpu.SemaphoreType.DMA
    vmem = pl.BlockSpec(memory_space=pltpu.VMEM)
    smem = pl.BlockSpec(memory_space=pltpu.SMEM)
    anys = pl.BlockSpec(memory_space=pl.ANY)
    held = lambda w: pltpu.VMEM(w.shape, w.dtype)
    out = pl.pallas_call(
        functools.partial(layer_kernel, A, B, G),
        out_shape=jax.ShapeDtypeStruct((n, D), f32),
        in_specs=[smem] * 2 + [vmem] * 6 + [anys] * 8,
        out_specs=vmem,
        scratch_shapes=[
            held(q_weight), held(k_weight), held(v_weight), held(o_weight),
            held(w_gate), held(w_up), held(w_down),
            pltpu.VMEM((G, 2, cs, kw), bf16),
            pltpu.VMEM((cs, kw), bf16), pltpu.VMEM((cs, kw), bf16),
            pltpu.VMEM((n, qw), bf16), pltpu.VMEM((n, kw), bf16), pltpu.VMEM((n, kw), bf16),
            pltpu.VMEM((n, D), f32), pltpu.VMEM((n, qw), f32), pltpu.VMEM((n, qw), f32),
            dma((8,)), dma((G,)), dma((G,)),
            pltpu.VMEM((pairs, 2 * R, D), bf16),
            block(pairs), block(pairs), block(pairs), block(pairs), block(pairs),
            block(A), block(A),
            dma((2 * pairs,)), dma((2 * pairs,)),
            dma((pairs,)), dma((pairs,)), dma((pairs,)), dma((pairs,)),
            dma((A,)), dma((A,)),
        ],
        compiler_params=pltpu.CompilerParams(
            collective_id=0, has_side_effects=True, vmem_limit_bytes=58 * 2**20
        ),
    )(
        cache_len, holder, accept, tokens[0], cosine, sine, attn_gain[None], ffn_gain[None],
        cache_kv[0], q_weight, k_weight, v_weight, o_weight, w_gate, w_up, w_down,
    )
    return out[None]


def solution(mesh):
    return jax.shard_map(
        functools.partial(local, dict(mesh.shape)),
        mesh=mesh,
        in_specs=(
            P(("req", "blk"), None, None),
            P(("req", "blk"), None, None, None),
            P(("req", "blk")),
            P(("req", "blk")),
            P(("req", "blk"), None),
            P(),
            P(),
            P(),
            P(),
            P(),
            P(),
            P(None, "blk"),
            P(None, "blk"),
            P("blk", None),
        ),
        out_specs=P(("req", "blk"), None, None),
        check_vma=False,
    )
```

time: 120 us -> 81.7 us (0.68)
  matrix products: 24.7 us -> 0 us
  Pallas kernels: 58.5 us -> 73.1 us
  blocking collectives: 13 us -> 0 us
  local copies, waits for them, and re-layouts: 13.7 us -> 4.65 us
  other arithmetic: 7.17 us -> 2.34 us
    dot_general x13 -> x0, matrix products: 20.7 us -> none  [the longest x6 10.7 us: project(): return jnp.dot(rows, weight, preferred_element_type=f32)]
    pallas_call x1, Pallas kernels: 58.5 us -> 73.1 us  [local(): pl.pallas_call(functools.partial(layer_kernel, A, B, G), out_shape=jax.Sh...]
    all_gather x1 -> x0, blocking collectives: 13 us -> none  [local(): slots = lax.all_gather(cache_kv, 'req', axis=0, tiled=True)]
    slice x8 -> x0, local copies, waits for them, and re-layouts: 5.21 us -> none  [the longest x3 1.7 us: local(): cache_keys, cache_vals = (fetched[0], fetched[1])]
    sub x2 -> x0, matrix products: 3.94 us -> none  [attend(): expd = jnp.exp(scores - peaks)]
    convert_element_type x4 -> x0, local copies, waits for them, and re-layouts: 3.6 us -> none  [the longest x1 1.64 us: local(): v1 = project(normed, v_weight).astype(bf16)]
    broadcast_in_dim x0 -> x2, local copies, waits for them, and re-layouts: none -> 2.58 us  [the longest x1 1.29 us: local(): ffn_gain[None]]
    mul x0 -> x1, other arithmetic: none -> 2.32 us  [local(): sine = jnp.where(lane < half, -1.0, 1.0) * jnp.sin(angles)]
where the time goes in v2:
time: 81.7 us; the launch traced here: 81.5 us
  Pallas kernels  73.1 us (89%)
  local copies, waits for them, and re-layouts  4.65 us (6%)
  other arithmetic  2.34 us (3%)
  between operations  1.31 us (2%)
    pallas_call x1, Pallas kernels, local(): pl.pallas_call(functools.partial(layer_kernel, A, B, G), out_shape=jax.Sh...  73.1 us
    mul x1, other arithmetic, local(): sine = jnp.where(lane < half, -1.0, 1.0) * jnp.sin(angles)  2.32 us
    unnamed x1, local copies, waits for them, and re-layouts  2.07 us

profile of v2, /device:TPU:0, one launch (start us, length us, event | category | flops | bytes accessed | tf_op | source)
XLA Modules:
  0.0 81.5 jit_solution(8430299654811719368)
XLA Ops:
  1.3 1.3 %broadcast_in_dim.22.again_ref = f32[1,1536]{1,0:T(1,128)} reshape(f32[1536]{0:T(1024)} %param.19) | data formatting | bytes 12288 | tf_op jit(solution)/shard_map/broadcast_in_dim | solution.py:359
  2.6 1.3 %broadcast_in_dim.23.fgain_ref = f32[1,1536]{1,0:T(1,128)} reshape(f32[1536]{0:T(1024)} %param.24) | data formatting | bytes 12288 | tf_op jit(solution)/shard_map/broadcast_in_dim | solution.py:359
  3.9 2.3 %fusion = (f32[128,768]{1,0:T(8,128)}, f32[128,768]{1,0:T(8,128)}) fusion(f32[768]{0:T(1024)S(1)} %get-tuple-element.8, f32[768]{0:T(1024)S(1)} %get-tuple-element.7, f32[128]{0:T(128)S(1)} %add_convert_fusion), kind=kLoop, calls=%fused_computation.2 | loop fusion | flops 196608 | bytes 793088 | tf_op jit(solution)/shard_map/mul | solution.py:323
  6.2 73.1 %shard_map.136 = f32[128,1536]{1,0:T(8,128)} custom-call(s32[1]{0:T(128)} %copy.16.length_ref, s32[1]{0:T(128)S(6)} %copy.17.holder_ref, s32[1,128]{1,0:T(1,128)} %accept_ref.1, bf16[128,1536]{1,0:T(8,128)(2,1)} %bitcast.6, f32[128,768]{1,0:T(8,128)} %get-tuple-element.6.cos_ref, f32[128,768]{1,0:T(8,128)} %get-tuple-element.5.sin_ref, ...), custom_call_target="tpu_custom_call" | custom-call | tf_op jit(solution)/shard_map/pallas_call | solution.py:335
  79.4 2.1 %copy.18 = f32[1,128,1536]{2,1,0:T(8,128)} copy(f32[1,128,1536]{2,1,0:T(8,128)} %bitcast.5) | data formatting | bytes 1572864
  (2 shorter events, 0.0 us)

commit v3 on v2

--- a/solution.py
+++ b/solution.py
@@ -169,7 +169,7 @@
     length = length_ref[0]
     kw = kn_ref.shape[1]
 
-    normed = rms_scale(x_ref[...], again_ref[...]).astype(bf16)
+    normed = rms_scale(x_ref[...], again_ref[...][None]).astype(bf16)
     loads[0].wait()
     q_ref[...] = rotate(dot(normed, wq_ref[...]), cosp[...], sinp[...])
     loads[1].wait()
@@ -191,7 +191,7 @@
     loads[4].wait()
     first = x_ref[:R] + dot(ctx, wo_ref[...])
     x_ref[:R] = first
-    ag[0, pl.ds(0, R)] = rms_scale(first, fgain_ref[...]).astype(bf16)
+    ag[0, pl.ds(0, R)] = rms_scale(first, fgain_ref[...][None]).astype(bf16)
 
     up_steps = A // 2
     down_steps = A - 1 - up_steps
@@ -282,7 +282,7 @@
         total = total + z_land[ra].astype(jnp.float32)
     draft = x_ref[:R] + total
     x_ref[:R] = draft
-    normed = rms_scale(draft, again_ref[...]).astype(bf16)
+    normed = rms_scale(draft, again_ref[...][None]).astype(bf16)
     q_ref[:R] = rotate(dot(normed, wq_ref[...]), cosp[:R], sinp[:R])
     kn_ref[:R] = rotate(dot(normed, wk_ref[...]), cosp[:R, :kw], sinp[:R, :kw])
     vn_ref[:R] = dot(normed, wv_ref[...]).astype(bf16)
@@ -356,7 +356,7 @@
             collective_id=0, has_side_effects=True, vmem_limit_bytes=58 * 2**20
         ),
     )(
-        cache_len, holder, accept, tokens[0], cosine, sine, attn_gain[None], ffn_gain[None],
+        cache_len, holder, accept, tokens[0], cosine, sine, attn_gain, ffn_gain,
         cache_kv[0], q_weight, k_weight, v_weight, o_weight, w_gate, w_up, w_down,
     )
     return out[None]

time: 81.7 us -> 79 us (0.967)
  local copies, waits for them, and re-layouts: 4.65 us -> 2.07 us
    broadcast_in_dim x2 -> x0, local copies, waits for them, and re-layouts: 2.58 us -> none  [the longest x1 1.29 us: local(): ffn_gain[None]]
where the time goes in v3:
time: 79 us; the launch traced here: 78.9 us
  Pallas kernels  73.1 us (93%)
  other arithmetic  2.35 us (3%)
  local copies, waits for them, and re-layouts  2.07 us (3%)
  between operations  1.31 us (2%)
    pallas_call x1, Pallas kernels, local(): pl.pallas_call(functools.partial(layer_kernel, A, B, G), out_shape=jax.Sh...  73.1 us
    mul x1, other arithmetic, local(): sine = jnp.where(lane < half, -1.0, 1.0) * jnp.sin(angles)  2.32 us
    unnamed x1, local copies, waits for them, and re-layouts  2.07 us

profile of v3, /device:TPU:0, one launch (start us, length us, event | category | flops | bytes accessed | tf_op | source)
XLA Modules:
  0.0 78.9 jit_solution(14434441680025793201)
XLA Ops:
  1.3 2.3 %fusion = (f32[128,768]{1,0:T(8,128)}, f32[128,768]{1,0:T(8,128)}) fusion(f32[768]{0:T(1024)S(1)} %get-tuple-element.8, f32[768]{0:T(1024)S(1)} %get-tuple-element.7, f32[128]{0:T(128)S(1)} %add_convert_fusion), kind=kLoop, calls=%fused_computation.2 | loop fusion | flops 196608 | bytes 793088 | tf_op jit(solution)/shard_map/mul | solution.py:323
  3.7 73.1 %shard_map.136 = f32[128,1536]{1,0:T(8,128)} custom-call(s32[1]{0:T(128)} %copy.16.length_ref, s32[1]{0:T(128)S(6)} %copy.17.holder_ref, s32[1,128]{1,0:T(1,128)} %accept_ref.1, bf16[128,1536]{1,0:T(8,128)(2,1)} %bitcast.6, f32[128,768]{1,0:T(8,128)} %get-tuple-element.6.cos_ref, f32[128,768]{1,0:T(8,128)} %get-tuple-element.5.sin_ref, f32[1536]{0:T(1024)} %again_ref.1, ...), custom_call_target="tpu_custom_call" | custom-call | tf_op jit(solution)/shard_map/pallas_call | solution.py:335
  76.8 2.1 %copy.18 = f32[1,128,1536]{2,1,0:T(8,128)} copy(f32[1,128,1536]{2,1,0:T(8,128)} %bitcast.5) | data formatting | bytes 1572864
  (2 shorter events, 0.0 us)
